TPU v7x, 256 devices: a whole 4x4x8 slice. The times are simulated.
256 devices in a mesh: seq: 2 (over core), row: 8 (over x, z_hi), col: 16 (over z_lo, y).
Axes of the slice: x: 4, y: 4, z: 8 (z_hi: 2, z_lo: 4; z = z_hi * 4 + z_lo), core: 2. Of those that a mesh axis runs over, the one named last changes fastest.
Arguments:
- first_linear_features: bfloat16 [256, 1536, 32], P('seq', ('row', 'col')), may hold values from -10 to 10
- second_linear_features: bfloat16 [256, 1536, 32], P('seq', ('col', 'row')), may hold values from -10 to 10
- coverage_indicator: int32 [256, 1536], replicated, may hold values from 0 to 1, as said below
- final_linear_matrix: bfloat16 [1024, 128], replicated, may hold values from -0.1875 to 0.1875
- final_offset_vector: float32 [128], replicated, may hold values from -6 to 6
Outputs:
- pair_delta_update: bfloat16 [1536, 1536, 128], P('row', ('col', 'seq'))
Inputs may be any that keep to these rules, and one draw needn't show every extreme that they name: `coverage_indicator`: each entry is 0 or 1; some residues are masked in every sequence.
All inputs are finite; a program needn't handle non-finite values.
Results may differ from a plain program's by a relative error of at most 0.0044.
Values may be sent and summed in bfloat16 or wider, within the bound.
A program may use at most 128 MiB of HBM per device.

v0:
```python
import math

import jax
import jax.numpy as jnp
from jax import lax
from jax.sharding import PartitionSpec as P


def pair_rows(a_block, b_block, final_linear_matrix):
    seq_count, row_count, chan_count = a_block.shape
    col_count = b_block.shape[1]
    product = lax.dot_general(
        a_block.reshape(seq_count, row_count * chan_count),
        b_block.reshape(seq_count, col_count * chan_count),
        (((0,), (0,)), ((), ())),
        preferred_element_type=jnp.float32,
    )
    product = product.reshape(row_count, chan_count, col_count, chan_count).transpose(0, 2, 1, 3)
    product = product.reshape(row_count * col_count, chan_count * chan_count).astype(jnp.bfloat16)
    return jnp.dot(product, final_linear_matrix, preferred_element_type=jnp.float32).reshape(
        row_count, col_count, final_linear_matrix.shape[1]
    )


def project_pairs(first_factor_zeroed, second_factor_zeroed, final_linear_matrix, row_step):
    seq_total, row_count, chan_count = first_factor_zeroed.shape
    col_count = second_factor_zeroed.shape[1]

    def one_slab(slab_index):
        a_slab = lax.dynamic_slice_in_dim(first_factor_zeroed, slab_index * row_step, row_step, 1)
        return pair_rows(a_slab, second_factor_zeroed, final_linear_matrix)

    slab_out = lax.map(one_slab, jnp.arange(row_count // row_step, dtype=jnp.int32))
    running = slab_out.reshape(row_count, col_count, final_linear_matrix.shape[1])
    return running


def local(
    first_linear_features,
    second_linear_features,
    coverage_indicator,
    final_linear_matrix,
    final_offset_vector,
):
    seq_index = lax.axis_index("seq")
    seq_parts = lax.axis_size("seq")
    first_factor_lines = lax.all_gather(first_linear_features, "col", axis=1, tiled=True)
    second_factor_lines = lax.all_gather(second_linear_features, "row", axis=1, tiled=True)
    local_seqs, row_count, chan_count = first_factor_lines.shape
    col_count = second_factor_lines.shape[1]
    col_width = col_count // seq_parts
    row_first = lax.axis_index("row") * row_count
    block_first = lax.axis_index("col") * col_count
    col_first = block_first + seq_index * col_width
    coverage_flags = coverage_indicator.astype(jnp.bfloat16)
    row_mask = lax.dynamic_slice_in_dim(coverage_flags, row_first, row_count, 1)
    col_mask = lax.dynamic_slice_in_dim(coverage_flags, col_first, col_width, 1)
    row_step = math.gcd(row_count, 32)
    seq_first = seq_index * local_seqs
    mine_rows = lax.dynamic_slice_in_dim(row_mask, seq_first, local_seqs, 0)
    sequence_block_mask = lax.dynamic_slice(
        coverage_flags, (seq_first, block_first), (local_seqs, col_count)
    )
    partial_sum = project_pairs(
        first_factor_lines * mine_rows[:, :, None],
        second_factor_lines * sequence_block_mask[:, :, None],
        final_linear_matrix,
        row_step,
    )
    summed = lax.psum_scatter(partial_sum, "seq", scatter_dimension=1, tiled=True)
    counts = lax.dot_general(
        row_mask, col_mask, (((0,), (0,)), ((), ())), preferred_element_type=jnp.float32
    )
    return ((summed + final_offset_vector) / jnp.maximum(counts, 1.0)[:, :, None]).astype(
        jnp.bfloat16
    )


def solution(mesh):
    in_specs = (P("seq", ("row", "col"), None), P("seq", ("col", "row"), None), P(), P(), P())
    out_specs = P("row", ("col", "seq"), None)
    return jax.shard_map(local, mesh=mesh, in_specs=in_specs, out_specs=out_specs, check_vma=False)
```

profile of v0, /device:TPU:1, one launch (start us, length us, event | category | flops | bytes accessed | tf_op | source)
XLA Modules:
  0.0 281.4 jit_solution(17641771381846102189)
XLA Ops:
  9.3 59.9 %all_gather.7 = bf16[128,96,32]{0,2,1:T(8,128)(2,1)S(1)} all-gather(bf16[128,12,32]{0,2,1:T(8,128)(2,1)} %param.8), channel_id=1, replica_groups=mesh['seq'=2,'row'=8,'col'=16] {'row'}, dimensions={1}, use_global_device_ids=true | all-gather | bytes 884736 | tf_op jit(solution)/shard_map/all_gather | solution.py:48
  69.2 22.1 %all-gather.2.cloned.1.call-done = bf16[128,192,32]{0,2,1:T(8,128)(2,1)} async-done(((bf16[128,12,32]{0,2,1:T(8,128)(2,1)}), bf16[128,192,32]{0,2,1:T(8,128)(2,1)}) %all-gather.2.cloned.1.call-update) | async-done | bytes 1572880 | tf_op jit(solution)/shard_map/all_gather | solution.py:47
  91.3 1.5 broadcast_multiply_fusion
  92.8 147.6 %while.10 = (s32[]{:T(128)}, f32[6,32,96,128]{3,2,1,0:T(8,128)}, s32[6]{0:T(128)S(1)}, bf16[128,192,32]{0,2,1:T(8,128)(2,1)S(1)}, bf16[128,96,32]{0,2,1:T(8,128)...) while((s32[]{:T(128)}, f32[6,32,96,128]{3,2,1,0:T(8,128)}, ...), condition=%wide.region_1.2_spmd, body=%wide.region_0.1_spmd.sunk | while | flops 1613758464 | bytes 30146736 | solution.py:33
  94.2 5.7 %convert_bitcast_fusion.2 = bf16[32,96,32,32]{1,2,3,0:T(8,128)(2,1)} fusion(bf16[96,32,128]{2,1,0:T(8,128)(2,1)S(1)} %bitcast.49, bf16[128,192,32]{0,2,1:T(8,128)(2,1)S(1)} %get-tuple-element.110, s32[]{:T(128)S(6)} %select_n.27), kind=kOutput, calls=%fused_computation.clone.1 | convolution fusion | flops 808452096 | bytes 7340036 | tf_op jit(solution)/shard_map/while/body/eval_jaxpr/dot_general | solution.py:12
  99.9 10.6 %copy.30 = bf16[32,96,32,32]{1,3,2,0:T(8,128)(2,1)} copy(bf16[32,96,32,32]{1,2,3,0:T(8,128)(2,1)} %convert_bitcast_fusion.2) | data formatting | bytes 12582912 | tf_op jit(solution)/shard_map/while/body/eval_jaxpr/convert_element_type | solution.py:19
  110.5 6.9 %bitcast_dynamic-update-slice_fusion.2 = f32[6,32,96,128]{3,2,1,0:T(8,128)} fusion(f32[6,32,96,128]{3,2,1,0:T(8,128)} %get-tuple-element.98, s32[]{:T(128)S(6)} %copy.34, bf16[32,96,1024]{1,2,0:T(8,128)(2,1)} %bitcast.48, bf16[1024,128]{1,0:T(8,128)(2,1)S(1)} %get-tuple-element.112), kind=kOutput, calls=%fused_computation.1.clone.1 | convolution fusion | flops 805306368 | bytes 10223620 | tf_op jit(solution)/shard_map/while/body/eval_jaxpr/dot_general | solution.py:20
  118.8 5.7 %convert_bitcast_fusion.2 = bf16[32,96,32,32]{1,2,3,0:T(8,128)(2,1)} fusion(bf16[96,32,128]{2,1,0:T(8,128)(2,1)S(1)} %bitcast.49, bf16[128,192,32]{0,2,1:T(8,128)(2,1)S(1)} %get-tuple-element.110, s32[]{:T(128)S(6)} %select_n.27), kind=kOutput, calls=%fused_computation.clone.1 | convolution fusion | flops 808452096 | bytes 7340036 | tf_op jit(solution)/shard_map/while/body/eval_jaxpr/dot_general | solution.py:12
  124.5 10.6 %copy.30 = bf16[32,96,32,32]{1,3,2,0:T(8,128)(2,1)} copy(bf16[32,96,32,32]{1,2,3,0:T(8,128)(2,1)} %convert_bitcast_fusion.2) | data formatting | bytes 12582912 | tf_op jit(solution)/shard_map/while/body/eval_jaxpr/convert_element_type | solution.py:19
  135.1 6.9 %bitcast_dynamic-update-slice_fusion.2 = f32[6,32,96,128]{3,2,1,0:T(8,128)} fusion(f32[6,32,96,128]{3,2,1,0:T(8,128)} %get-tuple-element.98, s32[]{:T(128)S(6)} %copy.34, bf16[32,96,1024]{1,2,0:T(8,128)(2,1)} %bitcast.48, bf16[1024,128]{1,0:T(8,128)(2,1)S(1)} %get-tuple-element.112), kind=kOutput, calls=%fused_computation.1.clone.1 | convolution fusion | flops 805306368 | bytes 10223620 | tf_op jit(solution)/shard_map/while/body/eval_jaxpr/dot_general | solution.py:20
  143.4 5.7 %convert_bitcast_fusion.2 = bf16[32,96,32,32]{1,2,3,0:T(8,128)(2,1)} fusion(bf16[96,32,128]{2,1,0:T(8,128)(2,1)S(1)} %bitcast.49, bf16[128,192,32]{0,2,1:T(8,128)(2,1)S(1)} %get-tuple-element.110, s32[]{:T(128)S(6)} %select_n.27), kind=kOutput, calls=%fused_computation.clone.1 | convolution fusion | flops 808452096 | bytes 7340036 | tf_op jit(solution)/shard_map/while/body/eval_jaxpr/dot_general | solution.py:12
  149.1 10.6 %copy.30 = bf16[32,96,32,32]{1,3,2,0:T(8,128)(2,1)} copy(bf16[32,96,32,32]{1,2,3,0:T(8,128)(2,1)} %convert_bitcast_fusion.2) | data formatting | bytes 12582912 | tf_op jit(solution)/shard_map/while/body/eval_jaxpr/convert_element_type | solution.py:19
  159.7 6.9 %bitcast_dynamic-update-slice_fusion.2 = f32[6,32,96,128]{3,2,1,0:T(8,128)} fusion(f32[6,32,96,128]{3,2,1,0:T(8,128)} %get-tuple-element.98, s32[]{:T(128)S(6)} %copy.34, bf16[32,96,1024]{1,2,0:T(8,128)(2,1)} %bitcast.48, bf16[1024,128]{1,0:T(8,128)(2,1)S(1)} %get-tuple-element.112), kind=kOutput, calls=%fused_computation.1.clone.1 | convolution fusion | flops 805306368 | bytes 10223620 | tf_op jit(solution)/shard_map/while/body/eval_jaxpr/dot_general | solution.py:20
  168.0 5.7 %convert_bitcast_fusion.2 = bf16[32,96,32,32]{1,2,3,0:T(8,128)(2,1)} fusion(bf16[96,32,128]{2,1,0:T(8,128)(2,1)S(1)} %bitcast.49, bf16[128,192,32]{0,2,1:T(8,128)(2,1)S(1)} %get-tuple-element.110, s32[]{:T(128)S(6)} %select_n.27), kind=kOutput, calls=%fused_computation.clone.1 | convolution fusion | flops 808452096 | bytes 7340036 | tf_op jit(solution)/shard_map/while/body/eval_jaxpr/dot_general | solution.py:12
  173.7 10.6 %copy.30 = bf16[32,96,32,32]{1,3,2,0:T(8,128)(2,1)} copy(bf16[32,96,32,32]{1,2,3,0:T(8,128)(2,1)} %convert_bitcast_fusion.2) | data formatting | bytes 12582912 | tf_op jit(solution)/shard_map/while/body/eval_jaxpr/convert_element_type | solution.py:19
  184.3 6.9 %bitcast_dynamic-update-slice_fusion.2 = f32[6,32,96,128]{3,2,1,0:T(8,128)} fusion(f32[6,32,96,128]{3,2,1,0:T(8,128)} %get-tuple-element.98, s32[]{:T(128)S(6)} %copy.34, bf16[32,96,1024]{1,2,0:T(8,128)(2,1)} %bitcast.48, bf16[1024,128]{1,0:T(8,128)(2,1)S(1)} %get-tuple-element.112), kind=kOutput, calls=%fused_computation.1.clone.1 | convolution fusion | flops 805306368 | bytes 10223620 | tf_op jit(solution)/shard_map/while/body/eval_jaxpr/dot_general | solution.py:20
  192.5 5.7 %convert_bitcast_fusion.2 = bf16[32,96,32,32]{1,2,3,0:T(8,128)(2,1)} fusion(bf16[96,32,128]{2,1,0:T(8,128)(2,1)S(1)} %bitcast.49, bf16[128,192,32]{0,2,1:T(8,128)(2,1)S(1)} %get-tuple-element.110, s32[]{:T(128)S(6)} %select_n.27), kind=kOutput, calls=%fused_computation.clone.1 | convolution fusion | flops 808452096 | bytes 7340036 | tf_op jit(solution)/shard_map/while/body/eval_jaxpr/dot_general | solution.py:12
  198.3 10.6 %copy.30 = bf16[32,96,32,32]{1,3,2,0:T(8,128)(2,1)} copy(bf16[32,96,32,32]{1,2,3,0:T(8,128)(2,1)} %convert_bitcast_fusion.2) | data formatting | bytes 12582912 | tf_op jit(solution)/shard_map/while/body/eval_jaxpr/convert_element_type | solution.py:19
  208.9 6.9 %bitcast_dynamic-update-slice_fusion.2 = f32[6,32,96,128]{3,2,1,0:T(8,128)} fusion(f32[6,32,96,128]{3,2,1,0:T(8,128)} %get-tuple-element.98, s32[]{:T(128)S(6)} %copy.34, bf16[32,96,1024]{1,2,0:T(8,128)(2,1)} %bitcast.48, bf16[1024,128]{1,0:T(8,128)(2,1)S(1)} %get-tuple-element.112), kind=kOutput, calls=%fused_computation.1.clone.1 | convolution fusion | flops 805306368 | bytes 10223620 | tf_op jit(solution)/shard_map/while/body/eval_jaxpr/dot_general | solution.py:20
  217.1 5.7 %convert_bitcast_fusion.2 = bf16[32,96,32,32]{1,2,3,0:T(8,128)(2,1)} fusion(bf16[96,32,128]{2,1,0:T(8,128)(2,1)S(1)} %bitcast.49, bf16[128,192,32]{0,2,1:T(8,128)(2,1)S(1)} %get-tuple-element.110, s32[]{:T(128)S(6)} %select_n.27), kind=kOutput, calls=%fused_computation.clone.1 | convolution fusion | flops 808452096 | bytes 7340036 | tf_op jit(solution)/shard_map/while/body/eval_jaxpr/dot_general | solution.py:12
  222.8 10.6 %copy.30 = bf16[32,96,32,32]{1,3,2,0:T(8,128)(2,1)} copy(bf16[32,96,32,32]{1,2,3,0:T(8,128)(2,1)} %convert_bitcast_fusion.2) | data formatting | bytes 12582912 | tf_op jit(solution)/shard_map/while/body/eval_jaxpr/convert_element_type | solution.py:19
  233.4 7.0 %bitcast_dynamic-update-slice_fusion.2 = f32[6,32,96,128]{3,2,1,0:T(8,128)} fusion(f32[6,32,96,128]{3,2,1,0:T(8,128)} %get-tuple-element.98, s32[]{:T(128)S(6)} %copy.34, bf16[32,96,1024]{1,2,0:T(8,128)(2,1)} %bitcast.48, bf16[1024,128]{1,0:T(8,128)(2,1)S(1)} %get-tuple-element.112), kind=kOutput, calls=%fused_computation.1.clone.1 | convolution fusion | flops 805306368 | bytes 10223620 | tf_op jit(solution)/shard_map/while/body/eval_jaxpr/dot_general | solution.py:20
  240.8 29.7 %reduce-scatter.2.cloned.1.call-done = f32[192,48,128]{2,1,0:T(8,128)} async-done(((f32[192,96,128]{2,1,0:T(8,128)}), f32[192,48,128]{2,1,0:T(8,128)}) %reduce-scatter.2.cloned.1.call-update) | async-done | bytes 4718608 | tf_op jit(solution)/shard_map/reduce_scatter | solution.py:70
  270.5 4.1 %divide_convert_fusion = bf16[192,48,128]{2,1,0:T(8,128)(2,1)} fusion(f32[192,48,128]{2,1,0:T(8,128)} %reduce-scatter.2.cloned.1.call-done, f32[192,48]{1,0:T(8,128)S(1)} %copy.20, f32[128]{0:T(128)S(1)} %copy-done.1), kind=kLoop, calls=%fused_computation.8 | loop fusion | flops 3538944 | bytes 7115264 | tf_op jit(solution)/shard_map/convert_element_type | solution.py:74
  (24 shorter events, 7.1 us)
Async XLA Ops:
  6.5 86.3 %copy-start = (bf16[1024,128]{1,0:T(8,128)(2,1)S(1)}, bf16[1024,128]{1,0:T(8,128)(2,1)}, u32[]{:S(2)}) copy-start(bf16[1024,128]{1,0:T(8,128)(2,1)} %param.10) | copy-start | bytes 786436
  6.5 84.7 %all-gather.2.cloned.1.call-start = ((), (), s32[]{:S(2)}) async-start(), calls=%async_computation.1 | async-start | bytes 1671168 | tf_op jit(solution)/shard_map/all_gather | solution.py:47
  7.3 263.2 %reduce-scatter.2.cloned.1.call-start = ((), (), s32[]{:S(2)}) async-start(), calls=%async_computation.2 | async-start | bytes 14155776 | tf_op jit(solution)/shard_map/reduce_scatter | solution.py:70
  240.4 30.1 %copy-start.1 = (f32[128]{0:T(128)S(1)}, f32[128]{0:T(128)}, u32[]{:S(2)}) copy-start(f32[128]{0:T(128)} %param.11) | copy-start | bytes 1540
Sparse Core Ops, SparseCore 0:
  9.1 82.0 all-gather.1
  240.6 29.8 reduce-scatter.1
where the time goes:
time: 282 us; the launch traced here: 281 us
  matrix products  76.1 us (27%)
  local copies, waits for them, and re-layouts  68 us (24%)
  blocking collectives  59.9 us (21%)
  waiting for transfers between devices  52.4 us (19%)
  between operations  13.5 us (5%)
  other arithmetic  7.17 us (3%)
  loops' own time  4.22 us (1%)
    convert_element_type x6, local copies, waits for them, and re-layouts, pair_rows(): product.reshape(row_count * col_count, chan_count * chan_count)  63.6 us
    all_gather x1, blocking collectives, local(): lax.all_gather(second_linear_features, 'row', axis=1, tiled=True)  59.9 us
    dot_general x6, matrix products, pair_rows(): jnp.dot(product, final_linear_matrix, preferred_element_type=jnp.float32)  41.5 us
    dot_general x6, matrix products, pair_rows(): lax.dot_general(a_block.reshape(seq_count, row_count * chan_count), b_blo...  34.4 us
    reduce_scatter x1, waiting for transfers between devices, local(): lax.psum_scatter(partial_sum, 'seq', scatter_dimension=1, tiled=True)  29.7 us
    all_gather x1, waiting for transfers between devices, local(): lax.all_gather(first_linear_features, 'col', axis=1, tiled=True)  22.1 us
  transfers between devices with their start and end apart: 2, of which 2 were waited for; matrix products, arithmetic and copies ran while one was open for 1% of the time, Pallas kernels for 0%

commit v1 on v0

v1 whole, which is shorter than its diff:
```python
import functools

import jax
import jax.numpy as jnp
from jax import lax
from jax.experimental import pallas as pl
from jax.experimental.pallas import tpu as pltpu
from jax.sharding import PartitionSpec as P

MESH = pl.DeviceIdType.MESH
F32 = jnp.float32
BF16 = jnp.bfloat16

CHAN = 32
BLK = 12
ROWS = BLK * CHAN
LANES = 128
NJ = 48
SLAB = 48
CZ = 128


def when_all(*conds):
    c = conds[0]
    for d in conds[1:]:
        c = jnp.logical_and(c, d)
    return pl.when(c)


def kernel(
    a_hbm, b_hbm, m_hbm, w_hbm, bias_ref, o_hbm,
    a_all, b_all, a_own, b_own, b_far, m_i, m_j, mt_i, mt_j, w_in, f_tmp, b_rot, w_rot, pairs, rcs, o_buf,
    load_sem, out_sem,
    bsend, brecv, fsend, frecv, zsend, zrecv, ysend, yrecv, csend, crecv,
):
    k = lax.axis_index("seq")
    row = lax.axis_index("row")
    col = lax.axis_index("col")
    x, zh = row // 2, row % 2
    zl, y = col // 4, col % 4
    half = x // 2
    yp, ym = (y + 1) % 4, (y + 3) % 4

    i_first = row * 192
    j_first = col * 96
    i_win = pl.multiple_of((i_first // 128) * 128, 128)
    j_win = pl.multiple_of(jnp.minimum((j_first // 128) * 128, 1280), 128)
    loads = [
        pltpu.make_async_copy(m_hbm.at[:, pl.ds(i_win, 256)], m_i, load_sem.at[0]),
        pltpu.make_async_copy(m_hbm.at[:, pl.ds(j_win, 256)], m_j, load_sem.at[1]),
        pltpu.make_async_copy(a_hbm, a_own, load_sem.at[2]),
        pltpu.make_async_copy(b_hbm, b_own, load_sem.at[3]),
        pltpu.make_async_copy(w_hbm, w_in, load_sem.at[4]),
    ]
    for c in loads:
        c.start()

    barrier = pltpu.get_barrier_semaphore()
    peers = [(1 - k, row, col), (k, row ^ 1, col)]
    for dx in (1, 2, 3):
        peers += [(s, row ^ (2 * dx), col) for s in (0, 1)]
    peers += [(k, row, col ^ (4 * g)) for g in (1, 2, 3)]
    peers += [(k, row, zl * 4 + yp), (k, row, zl * 4 + ym)]
    for p in peers:
        pl.semaphore_signal(barrier, inc=1, device_id=p, device_id_type=MESH)

    loads[0].wait()
    for s in range(2):
        mt_i[s] = m_i[pl.ds(s * LANES, LANES), :].astype(F32).T
    loads[1].wait()
    for s in range(2):
        mt_j[s] = m_j[pl.ds(s * LANES, LANES), :].astype(F32).T
    loads[3].wait()
    jo = j_first + row * BLK - j_win
    for n in range(BLK):
        flags = mt_j[k, pl.ds(jo + n, 1), :].astype(BF16)
        sl = pl.ds(n * CHAN, CHAN)
        b_own[sl, :] = b_own[sl, :] * flags
    loads[2].wait()
    io = i_first + col * BLK - i_win
    for n in range(BLK):
        flags = mt_i[k, pl.ds(io + n, 1), :].astype(BF16)
        sl = pl.ds(n * CHAN, CHAN)
        a_all[col, k, sl, :] = a_own[sl, :] * flags

    pl.semaphore_wait(barrier, len(peers))

    HALF = ROWS // 2
    far = [
        pltpu.make_async_remote_copy(
            src_ref=b_own.at[pl.ds(h * HALF, HALF)],
            dst_ref=b_far.at[pl.ds(h * HALF, HALF)],
            send_sem=fsend.at[h],
            recv_sem=frecv.at[h],
            device_id=(k, row ^ 1, col),
            device_id_type=MESH,
        )
        for h in range(2)
    ]

    def b_copy(origin, h, dx):
        src = (b_own, b_far)[origin].at[pl.ds(h * HALF, HALF)]
        slot = (x % 2) * 2 + (zh if origin == 0 else 1 - zh)
        dst = b_all.at[slot, k, pl.ds(h * HALF, HALF)]
        return src, dst, brecv.at[slot, k, h]

    def b_spread(origin, h):
        for dx in (1, 3, 2):
            src, dst, sem = b_copy(origin, h, dx)
            pltpu.make_async_remote_copy(
                src_ref=src, dst_ref=dst, send_sem=bsend.at[origin, h, dx], recv_sem=sem,
                device_id=(half, row ^ (2 * dx), col), device_id_type=MESH,
            ).start()
        src, dst, sem = b_copy(origin, h, 0)

        @pl.when(half == k)
        def _():
            pltpu.make_async_copy(src, dst, sem).start()

        @pl.when(half != k)
        def _():
            pltpu.make_async_remote_copy(
                src_ref=src, dst_ref=dst, send_sem=bsend.at[origin, h, 0], recv_sem=sem,
                device_id=(1 - k, row, col), device_id_type=MESH,
            ).start()

    def b_drain():
        for origin in range(2):
            for h in range(2):
                for dx in range(4):
                    src, dst, sem = b_copy(origin, h, dx)

                    def done():
                        pltpu.make_async_copy(src, src, bsend.at[origin, h, dx]).wait()

                    if dx:
                        done()
                    else:
                        pl.when(half != k)(done)

    PIECES = ((0, ROWS), (0, ROWS), (0, ROWS), (0, HALF), (HALF, HALF))

    def a_piece(g, role, core):
        zg = zl ^ g
        yy = (y, ym, yp, (y + 2) % 4, (y + 2) % 4)[role]
        first, size = PIECES[role]
        return a_all.at[zg * 4 + yy, core, pl.ds(first, size)]

    def to_core(g, role):
        piece = a_piece(g, role, k)
        return pltpu.make_async_remote_copy(
            src_ref=piece, dst_ref=piece, send_sem=csend.at[g, role], recv_sem=crecv.at[g, role],
            device_id=(1 - k, row, col), device_id_type=MESH,
        )

    def to_z(g):
        mine = a_all.at[col, k]
        return pltpu.make_async_remote_copy(
            src_ref=mine, dst_ref=mine, send_sem=zsend.at[g - 1], recv_sem=zrecv.at[g - 1],
            device_id=(k, row, col ^ (4 * g)), device_id_type=MESH,
        )

    def to_y(g, what):
        zg = zl ^ g
        if what < 2:
            src = a_all.at[zg * 4 + y, k]
        elif what == 2:
            src = a_all.at[zg * 4 + ym, k, pl.ds(0, HALF)]
        else:
            src = a_all.at[zg * 4 + yp, k, pl.ds(HALF, HALF)]
        target = yp if what in (0, 2) else ym
        return pltpu.make_async_remote_copy(
            src_ref=src, dst_ref=src, send_sem=ysend.at[g, what], recv_sem=yrecv.at[g, what],
            device_id=(k, row, zl * 4 + target), device_id_type=MESH,
        )

    def arrived(piece, sem):
        pltpu.make_async_copy(piece, piece, sem).wait()

    def stage_a(g):
        if g:
            arrived(a_piece(g, 0, k), zrecv.at[g - 1])
        to_y(g, 0).start()
        to_y(g, 1).start()
        to_core(g, 0).start()

    def stage_b(g):
        arrived(a_piece(g, 1, k), yrecv.at[g, 0])
        to_y(g, 2).start()
        to_core(g, 1).start()
        arrived(a_piece(g, 2, k), yrecv.at[g, 1])
        to_y(g, 3).start()
        to_core(g, 2).start()

    def stage_c(g):
        arrived(a_piece(g, 3, k), yrecv.at[g, 2])
        to_core(g, 3).start()
        arrived(a_piece(g, 4, k), yrecv.at[g, 3])
        to_core(g, 4).start()

    for c in far:
        c.start()
    b_spread(0, 0)
    b_spread(0, 1)
    stage_a(0)
    for g in (1, 2, 3):
        to_z(g).start()

    loads[4].wait()
    f_tmp[0:1024, :] = w_in[...].astype(F32)
    for e in range(CHAN):
        e8, r = e // 4, e % 4
        part = f_tmp[pl.ds(e, CHAN, stride=CHAN), :].astype(BF16)
        for d in range(4):
            w_rot[d, pl.ds((e8 * 4 + (r + d) % 4) * CHAN, CHAN), :] = part

    jc = pl.multiple_of(j_first + k * NJ - j_win, 16)
    counts = lax.dot_general(
        jnp.concatenate([mt_j[s, pl.ds(jc, NJ), :] for s in range(2)], axis=1).astype(BF16),
        jnp.concatenate([mt_i[s] for s in range(2)], axis=1).astype(BF16),
        (((1,), (1,)), ((), ())),
        preferred_element_type=F32,
    )
    counts = jnp.where(i_first == i_win, counts[:, 0:192], counts[:, 64:256])
    recip = 1.0 / jnp.maximum(counts, 1.0)
    for z in range(4):
        rcs[z, :, 0:SLAB] = recip[:, z * SLAB:(z + 1) * SLAB]

    stage_b(0)
    stage_a(1)
    far[0].wait_recv()
    b_spread(1, 0)
    stage_b(1)
    far[1].wait_recv()
    b_spread(1, 1)
    stage_c(0)
    stage_a(2)
    stage_c(1)

    for slot in range(4):
        for s in range(2):
            for h in range(2):
                arrived(b_all.at[slot, s, pl.ds(h * HALF, HALF)], brecv.at[slot, s, h])
    for s in range(2):
        for slot in range(4):
            f_tmp[pl.ds(slot * ROWS, ROWS), :] = b_all[slot, s].astype(F32)
        for e in range(CHAN):
            e8, r = e // 4, e % 4
            part = f_tmp[pl.ds(e, NJ, stride=CHAN), :].astype(BF16)
            b_rot[r, pl.ds(e8 * NJ, NJ), pl.ds(s * LANES, LANES)] = part

    lane = lax.broadcasted_iota(jnp.int32, (NJ, 128), 1) // CHAN
    odd = (lane % 2) == 1
    high = lane >= 2
    bias = bias_ref[...]

    def slab(q, _):
        zg = zl ^ q
        for role in range(5):
            yy = (y, ym, yp, (y + 2) % 4, (y + 2) % 4)[role]
            first, size = PIECES[role]
            arrived(a_all.at[zg * 4 + yy, 1 - k, pl.ds(first, size)], crecv.at[q, role])

        for t in range(6):
            if t == 0:
                pl.when(q == 0)(lambda: stage_b(2))
            if t == 1:
                pl.when(q == 0)(lambda: stage_a(3))
            if t == 3:
                pl.when(q == 0)(lambda: stage_c(2))
            if t == 4:
                pl.when(q == 0)(lambda: stage_b(3))
            groups = []
            for h in range(2):
                chip, part = (t * 2 + h) // 3, (t * 2 + h) % 3
                groups.append([
                    jnp.concatenate(
                        [a_all[zg * 4 + chip, s, pl.ds(part * 128 + d * CHAN, CHAN), :] for s in range(2)], axis=1
                    )
                    for d in range(4)
                ])
            outer = []
            for r in range(4):
                rot = jnp.concatenate([grp[(g - r) % 4] for grp in groups for g in range(4)], axis=0)
                outer.append(
                    lax.dot_general(b_rot[r], rot, (((1,), (1,)), ((), ())), preferred_element_type=F32)
                )
            for h in range(2):
                rows = pl.ds((t * 2 + h) * NJ, NJ)
                for e8 in range(8):
                    v = [outer[r][e8 * NJ:(e8 + 1) * NJ, h * 128:(h + 1) * 128] for r in range(4)]
                    for d in range(4):
                        low = jnp.where(odd, v[(1 - d) % 4], v[(0 - d) % 4])
                        top = jnp.where(odd, v[(3 - d) % 4], v[(2 - d) % 4])
                        pairs[d, rows, pl.ds(e8 * 128, 128)] = jnp.where(high, top, low).astype(BF16)
        pl.when(q == 0)(lambda: stage_c(3))
        rc = rcs[zg]
        for d in range(4):
            acc = jnp.dot(pairs[d], w_rot[d], preferred_element_type=F32) + bias
            for grp in range(12):
                i = grp * 4 + d
                o_buf[zg * SLAB + i] = (acc[grp * NJ:(grp + 1) * NJ] * rc[:, i:i + 1]).astype(BF16)
        rows = pl.ds(zg * SLAB, SLAB)
        pltpu.make_async_copy(o_buf.at[rows], o_hbm.at[rows], out_sem.at[q]).start()
        return 0

    lax.fori_loop(0, 4, slab, 0)

    for c in far:
        c.wait_send()
    b_drain()
    for g in range(4):
        if g:
            to_z(g).wait_send()
        for what in range(4):
            to_y(g, what).wait_send()
        for role in range(5):
            to_core(g, role).wait_send()
    for q in range(4):
        rows = pl.ds((zl ^ q) * SLAB, SLAB)
        pltpu.make_async_copy(o_buf.at[rows], o_hbm.at[rows], out_sem.at[q]).wait()


def local(first, second, coverage, matrix, offset):
    seqs, block, chans = first.shape
    a = jnp.transpose(first, (1, 2, 0)).reshape(block * chans, seqs)
    b = jnp.transpose(second, (1, 2, 0)).reshape(block * chans, seqs)
    hbm = pl.BlockSpec(memory_space=pl.ANY)
    vmem = pl.BlockSpec(memory_space=pltpu.VMEM)
    dma = pltpu.SemaphoreType.DMA
    return pl.pallas_call(
        kernel,
        out_shape=jax.ShapeDtypeStruct((192, NJ, CZ), BF16),
        in_specs=[hbm, hbm, hbm, hbm, vmem],
        out_specs=hbm,
        scratch_shapes=[
            pltpu.VMEM((16, 2, ROWS, LANES), BF16),
            pltpu.VMEM((4, 2, ROWS, LANES), BF16),
            pltpu.VMEM((ROWS, LANES), BF16),
            pltpu.VMEM((ROWS, LANES), BF16),
            pltpu.VMEM((ROWS, LANES), BF16),
            pltpu.VMEM((256, 256), jnp.int32),
            pltpu.VMEM((256, 256), jnp.int32),
            pltpu.VMEM((2, 256, LANES), F32),
            pltpu.VMEM((2, 256, LANES), F32),
            pltpu.VMEM((1024, CZ), BF16),
            pltpu.VMEM((1536, 128), F32),
            pltpu.VMEM((4, 8 * NJ, 256), BF16),
            pltpu.VMEM((4, 1024, CZ), BF16),
            pltpu.VMEM((4, 12 * NJ, 1024), BF16),
            pltpu.VMEM((4, NJ, 128), F32),
            pltpu.VMEM((192, NJ, CZ), BF16),
            dma((5,)),
            dma((4,)),
            dma((2, 2, 4)),
            dma((4, 2, 2)),
            dma((2,)),
            dma((2,)),
            dma((3,)),
            dma((3,)),
            dma((4, 4)),
            dma((4, 4)),
            dma((4, 5)),
            dma((4, 5)),
        ],
        compiler_params=pltpu.CompilerParams(
            collective_id=0, has_side_effects=True, vmem_limit_bytes=56 * 2**20
        ),
        cost_estimate=pl.CostEstimate(flops=7 * 10**9, bytes_accessed=5 * 10**6, transcendentals=0),
    )(a, b, coverage, matrix, offset.reshape(1, CZ))


def solution(mesh):
    in_specs = (P("seq", ("row", "col"), None), P("seq", ("col", "row"), None), P(), P(), P())
    out_specs = P("row", ("col", "seq"), None)
    return jax.shard_map(local, mesh=mesh, in_specs=in_specs, out_specs=out_specs, check_vma=False)
```

time: 282 us -> 57.3 us (0.20)
  matrix products: 76.1 us -> 0 us
  local copies, waits for them, and re-layouts: 68 us -> 3.48 us
  blocking collectives: 59.9 us -> 0 us
  Pallas kernels: 0 us -> 53.6 us
  waiting for transfers between devices: 52.4 us -> 0 us
  between operations: 13.5 us -> 0.01 us
  other arithmetic: 7.17 us -> 0 us
  loops' own time: 4.22 us -> 0 us
    dot_general x13 -> x0, matrix products: 76.1 us -> none  [the longest x6 41.5 us: pair_rows(): jnp.dot(product, final_linear_matrix, preferred_element_type=jnp.float32)]
    convert_element_type x6 -> x0, local copies, waits for them, and re-layouts: 63.6 us -> none  [pair_rows(): product.reshape(row_count * col_count, chan_count * chan_count)]
    all_gather x1 -> x0, blocking collectives: 59.9 us -> none  [local(): lax.all_gather(second_linear_features, 'row', axis=1, tiled=True)]
    pallas_call x0 -> x1, Pallas kernels: none -> 53.6 us  [local(): pl.pallas_call(kernel, out_shape=jax.ShapeDtypeStruct((192, NJ, CZ), BF16...]
    reduce_scatter x1 -> x0, waiting for transfers between devices: 29.7 us -> none  [local(): lax.psum_scatter(partial_sum, 'seq', scatter_dimension=1, tiled=True)]
    all_gather x1 -> x0, waiting for transfers between devices: 22.1 us -> none  [local(): lax.all_gather(first_linear_features, 'col', axis=1, tiled=True)]
    convert_element_type x2 -> x0, other arithmetic: 5.58 us -> none  [the longest x1 4.07 us: local(): ((summed + final_offset_vector) / jnp.maximum(counts, 1.0)[:, :, None]).a...]
    dynamic_slice x10 -> x0, local copies, waits for them, and re-layouts: 4.36 us -> none  [the longest x6 3.95 us: project_pairs(): lax.map(one_slab, jnp.arange(row_count // row_step, dtype=jnp.int32))]
  transfers between devices with their start and end apart: 2 -> 0, of which waited for: 2 -> 0; matrix products, arithmetic and copies ran while one was open for 1% -> 0% of each run, Pallas kernels for 0% -> 0%
where the time goes in v1:
time: 57.3 us; the launch traced here: 57.1 us
  Pallas kernels  53.6 us (94%)
  local copies, waits for them, and re-layouts  3.48 us (6%)
    pallas_call x1, Pallas kernels, local(): pl.pallas_call(kernel, out_shape=jax.ShapeDtypeStruct((192, NJ, CZ), BF16...  53.6 us
    unnamed x1, local copies, waits for them, and re-layouts  3.48 us

profile of v1, /device:TPU:1, one launch (start us, length us, event | category | flops | bytes accessed | tf_op | source)
XLA Modules:
  0.0 57.1 jit_solution(14772621486744356127)
XLA Ops:
  0.0 53.6 %shard_map.55 = bf16[192,48,128]{2,1,0:T(8,128)(2,1)} custom-call(bf16[384,128]{1,0:T(8,128)(2,1)} %bitcast.7, bf16[384,128]{1,0:T(8,128)(2,1)} %bitcast.8, s32[256,1536]{1,0:T(8,128)} %m_hbm.1, bf16[1024,128]{1,0:T(8,128)(2,1)} %w_hbm.1, f32[1,128]{1,0:T(1,128)} %bitcast.9), custom_call_target="tpu_custom_call" | custom-call | flops 7000000000 | bytes 5000000 | tf_op jit(solution)/shard_map/pallas_call | solution.py:331
  53.6 3.5 %copy.7 = bf16[192,48,128]{2,1,0:T(8,128)(2,1)} copy(bf16[192,48,128]{2,1,0:T(8,128)(2,1)} %shard_map.55) | data formatting | bytes 4718592

commit v2 on v0

v2 whole, which is shorter than its diff:
```python
import jax
import jax.numpy as jnp
from jax import lax
from jax.experimental import pallas as pl
from jax.experimental.pallas import tpu as pltpu
from jax.sharding import PartitionSpec as P

MESH = pl.DeviceIdType.MESH
F32 = jnp.float32
BF16 = jnp.bfloat16

CHAN = 32
BLK = 12
ROWS = BLK * CHAN
PART = 4 * CHAN
HALF = PART // 2
LANES = 128
NJ = 48
CZ = 128
SPAN = 64
STRIDE = 56


def kernel(
    a_hbm, b_hbm, m_hbm, w_hbm, bias_hbm, o_ref,
    a_all, b_all, a_own, b_own, b_far, m_i, m_j, mt_i, mt_j, mt_a, w_in, bias_in, w_even_odd, perm, a_perm, b_split,
    outer, recip_tmp, recips, staged,
    load_sem, bsend, brecv, fsend, frecv, zsend, zrecv, ysend, yrecv, csend, crecv,
):
    k = lax.axis_index("seq")
    row = lax.axis_index("row")
    col = lax.axis_index("col")
    x, zh = row // 2, row % 2
    zl, y = col // 4, col % 4
    half = x // 2
    yp, ym = (y + 1) % 4, (y + 3) % 4

    i_first = row * 192
    j_first = col * 96
    i_win = pl.multiple_of((i_first // 128) * 128, 128)
    j_win = pl.multiple_of(jnp.minimum((j_first // 128) * 128, 1280), 128)
    loads = [
        pltpu.make_async_copy(m_hbm.at[:, pl.ds(i_win, 256)], m_i, load_sem.at[0]),
        pltpu.make_async_copy(m_hbm.at[:, pl.ds(j_win, 256)], m_j, load_sem.at[1]),
        pltpu.make_async_copy(a_hbm, a_own, load_sem.at[2]),
        pltpu.make_async_copy(b_hbm, b_own, load_sem.at[3]),
        pltpu.make_async_copy(w_hbm, w_in, load_sem.at[4]),
        pltpu.make_async_copy(bias_hbm, bias_in, load_sem.at[5]),
    ]
    for c in loads:
        c.start()

    barrier = pltpu.get_barrier_semaphore()
    peers = [(1 - k, row, col), (k, row ^ 1, col)]
    for dx in (1, 2, 3):
        peers += [(s, row ^ (2 * dx), col) for s in (0, 1)]
    peers += [(k, row, col ^ (4 * g)) for g in (1, 2, 3)]
    peers += [(k, row, zl * 4 + (y + dy) % 4) for dy in (1, 2, 3)]
    for p in peers:
        pl.semaphore_signal(barrier, inc=1, device_id=p, device_id_type=MESH)

    loads[0].wait()
    for s in range(2):
        mt_i[s] = m_i[pl.ds(s * LANES, LANES), :].astype(F32).T
    loads[1].wait()
    for s in range(2):
        mt_j[s] = m_j[pl.ds(s * LANES, LANES), :].astype(F32).T
    loads[3].wait()
    jo = j_first + row * BLK - j_win
    for n in range(BLK):
        flags = mt_j[k, pl.ds(jo + n, 1), :].astype(BF16)
        sl = pl.ds(n * CHAN, CHAN)
        b_own[sl, :] = b_own[sl, :] * flags
    loads[2].wait()
    i_off = pl.multiple_of(i_first - i_win, 64)
    for n in range(BLK):
        flags = mt_i[k, pl.ds(i_off + col * BLK + n, 1), :].astype(BF16)
        a_all[n // 4, k, 0, 0, pl.ds((n % 4) * CHAN, CHAN), :] = a_own[pl.ds(n * CHAN, CHAN), :] * flags

    pl.semaphore_wait(barrier, len(peers))

    far = [
        pltpu.make_async_remote_copy(
            src_ref=b_own.at[pl.ds(h * PART, PART)],
            dst_ref=b_far.at[pl.ds(h * PART, PART)],
            send_sem=fsend.at[h],
            recv_sem=frecv.at[h],
            device_id=(k, row ^ 1, col),
            device_id_type=MESH,
        )
        for h in range(3)
    ]

    def b_copy(h):
        rows = pl.ds(0, ROWS) if h is None else pl.ds(h * PART, PART)
        src = (b_own if h is None else b_far).at[rows]
        slot = (x % 2) * 2 + (zh if h is None else 1 - zh)
        dst = b_all.at[slot, k, rows]
        return src, dst, brecv.at[slot, k, h or 0], 3 if h is None else h

    def b_spread(h):
        src, dst, sem, n = b_copy(h)
        for dx in (2, 1, 3):
            pltpu.make_async_remote_copy(
                src_ref=src, dst_ref=dst, send_sem=bsend.at[n, dx], recv_sem=sem,
                device_id=(half, row ^ (2 * dx), col), device_id_type=MESH,
            ).start()

        @pl.when(half == k)
        def _():
            pltpu.make_async_copy(src, dst, sem).start()

        @pl.when(half != k)
        def _():
            pltpu.make_async_remote_copy(
                src_ref=src, dst_ref=dst, send_sem=bsend.at[n, 0], recv_sem=sem,
                device_id=(1 - k, row, col), device_id_type=MESH,
            ).start()

    def b_drain():
        for h in (None, 0, 1, 2):
            src, dst, sem, n = b_copy(h)
            for dx in range(4):

                def done():
                    pltpu.make_async_copy(src, src, bsend.at[n, dx]).wait()

                if dx:
                    done()
                else:
                    pl.when(half != k)(done)


    def remote(src, dst, send_sem, recv_sem, device):
        return pltpu.make_async_remote_copy(
            src_ref=src, dst_ref=dst, send_sem=send_sem, recv_sem=recv_sem, device_id=device, device_id_type=MESH
        )

    def to_core(r):
        piece = a_all.at[r, k]
        return remote(piece, piece, csend.at[r], crecv.at[r], (1 - k, row, col))

    def to_z(r, g):
        return remote(
            a_all.at[r, k, 0, 0], a_all.at[r, k, 0, g], zsend.at[r, g - 1], zrecv.at[r, g - 1], (k, row, col ^ (4 * g))
        )

    def to_y(r, rest, dy):
        sl = pl.ds(1, 3) if rest else pl.ds(0, 1)
        src, dst = a_all.at[r, k, 0, sl], a_all.at[r, k, dy, sl]
        target = zl * 4 + (yp, ym, (y + 2) % 4)[dy - 1]
        return remote(src, dst, ysend.at[r, rest, dy - 1], yrecv.at[r, rest, dy - 1], (k, row, target))

    def arrived(piece, sem):
        pltpu.make_async_copy(piece, piece, sem).wait()

    def z_send(r):
        to_z(r, 1).start()
        to_z(r, 2).start()

        to_z(r, 3).start()

    def stage_a(r):
        for g in (1, 2, 3):
            arrived(a_all.at[r, k, 0, g], zrecv.at[r, g - 1])
        for dy in (3, 1, 2):
            to_y(r, 1, dy).start()

    def stage_b(r):
        for dy in (1, 2, 3):
            arrived(a_all.at[r, k, dy, pl.ds(0, 1)], yrecv.at[r, 0, dy - 1])
            arrived(a_all.at[r, k, dy, pl.ds(1, 3)], yrecv.at[r, 1, dy - 1])
        to_core(r).start()

    def gathered(r):
        arrived(a_all.at[r, 1 - k], crecv.at[r])

    origin_col = [(zl ^ g) * 4 + yy for yy in (y, ym, yp, (y + 2) % 4) for g in range(4)]

    z_send(0)
    for c in far:
        c.start()
    for r in range(3):
        for dy in (3, 1, 2):
            to_y(r, 0, dy).start()
    b_spread(None)
    z_send(1)
    z_send(2)

    loads[4].wait()
    loads[5].wait()
    for odd in range(2):
        part = jnp.concatenate([w_in[pl.ds((2 * c + odd) * CHAN, CHAN), :] for c in range(16)], axis=0)
        w_even_odd[odd] = part.astype(F32).T.astype(BF16)
    bias = jnp.broadcast_to(bias_in[...], (CZ, CZ)).T
    out_row = lax.broadcasted_iota(jnp.int32, (256, 256), 0)
    in_row = lax.broadcasted_iota(jnp.int32, (256, 256), 1)
    perm[...] = (in_row == (out_row % 8) * CHAN + out_row // 8).astype(F32).astype(BF16)

    jc = pl.multiple_of(j_first + k * NJ - j_win, 16)
    flags_j = jnp.concatenate([mt_j[s, pl.ds(jc, NJ), :] for s in range(2)], axis=1).astype(BF16)
    for r in range(3):
        for s in range(2):
            for c in range(16):
                for n in range(4):
                    mt_a[s, pl.ds(c * 4 + n, 1), :] = mt_i[s, pl.ds(i_off + origin_col[c] * BLK + r * 4 + n, 1), :]
        flags_i = jnp.concatenate([mt_a[s] for s in range(2)], axis=1).astype(BF16)
        counts = lax.dot_general(flags_j, flags_i, (((1,), (1,)), ((), ())), preferred_element_type=F32)
        recip_tmp[:, 0:SPAN] = 1.0 / jnp.maximum(counts, 1.0)
        for odd in range(2):
            recips[r, :, pl.ds(odd * SPAN, SPAN)] = recip_tmp[pl.ds(odd, NJ // 2, stride=2), :][:, 0:SPAN]

    stage_a(0)
    stage_a(1)
    stage_a(2)
    for h in range(3):
        far[h].wait_recv()
        b_spread(h)
    stage_b(0)
    stage_b(1)

    def prepare_b():
        for xx in range(2):
            for s in range(2):
                arrived(b_all.at[xx * 2 + zh, s], brecv.at[xx * 2 + zh, s, 0])
        for h in range(3):
            for xx in range(2):
                for s in range(2):
                    slot = xx * 2 + 1 - zh
                    arrived(b_all.at[slot, s, pl.ds(h * PART, PART)], brecv.at[slot, s, h])
        for slot in range(4):
            for s in range(2):
                for n in range(BLK):
                    rows = pl.ds((slot * 6 + n // 2) * CHAN, CHAN)
                    b_split[n % 2, rows, pl.ds(s * LANES, LANES)] = b_all[slot, s, pl.ds(n * CHAN, CHAN), :]

    def prepare_a(r):
        for pair in range(4):
            moved = []
            for g in (2 * pair, 2 * pair + 1):
                block = jnp.concatenate(
                    [jnp.concatenate([a_all[r, s, g // 2, (2 * g + u) % 4] for s in range(2)], axis=1) for u in range(2)], axis=0
                )
                moved.append(jnp.dot(perm[...], block, preferred_element_type=F32))
            for c in range(CHAN):
                part = jnp.concatenate([v[c * 8:(c + 1) * 8] for v in moved], axis=0)
                a_perm[c, pl.ds(pair * 16, 16), :] = part.astype(BF16)

    def outer_step(ct):
        for odd in range(2):
            rows = []
            for c in (4 * ct, 4 * ct + 2):
                pair = [a_perm[c], a_perm[c + 1]]
                rows += pair[::-1] if odd else pair
            value = lax.dot_general(
                b_split[odd], jnp.concatenate(rows, axis=0), (((1,), (1,)), ((), ())), preferred_element_type=F32
            )
            outer[odd, :, pl.ds(ct * 256, 256)] = value.astype(BF16)

    def project_step(r, jp):
        low = lax.broadcasted_iota(jnp.int16, (CHAN, 128), 1) < SPAN
        left, right = [], []
        for u in range(2):
            rows = pl.ds((jp + u) * CHAN, CHAN)
            keep, swap = [], []
            for c in range(16):
                v0 = outer[0, rows, pl.ds(c * 128, 128)]
                v1 = outer[1, rows, pl.ds(c * 128, 128)]
                keep.append(jnp.where(low, v0, v1))
                swap.append(jnp.where(low, v1, v0))
            left.append(jnp.concatenate(keep, axis=0))
            right.append(jnp.concatenate(swap, axis=0))
        acc0 = jnp.dot(w_even_odd[0], jnp.concatenate(left, axis=1), preferred_element_type=F32)
        acc1 = jnp.dot(w_even_odd[1], jnp.concatenate(right, axis=1), preferred_element_type=F32)
        for u in range(2):
            lanes = slice(u * 128, (u + 1) * 128)
            value = acc0[:, lanes] + pltpu.roll(acc1[:, lanes], SPAN, 1) + bias
            value = (value * recips[r, pl.ds(jp + u, 1), :]).T
            j = 2 * (jp + u)
            staged[pl.ds(j, SPAN, stride=STRIDE), :] = value[0:SPAN]
            staged[pl.ds(j + 1, SPAN, stride=STRIDE), :] = value[SPAN:2 * SPAN]

    def finish(r):
        for c in range(16):
            for n in range(4):
                i = c * 4 + n
                o_ref[origin_col[c] * BLK + r * 4 + n] = staged[pl.ds(i * STRIDE, NJ), :].astype(BF16)

    events = {(0, 10): lambda: stage_b(2)}
    prepare_b()
    for r in range(3):
        gathered(r)
        prepare_a(r)
        for n in range(20):
            if n < 8:
                outer_step(n)
            else:
                project_step(r, 2 * (n - 8))
            if (r, n) in events:
                events[r, n]()
        finish(r)

    for c in far:
        c.wait_send()
    b_drain()
    for r in range(3):
        to_z(r, 1).wait_send()
        to_z(r, 2).wait_send()

        to_z(r, 3).wait_send()

        for rest in range(2):
            for dy in (1, 2, 3):
                to_y(r, rest, dy).wait_send()
        to_core(r).wait_send()


def local(first, second, coverage, matrix, offset):
    seqs, block, chans = first.shape
    a = jnp.transpose(first, (1, 2, 0)).reshape(block * chans, seqs)
    b = jnp.transpose(second, (1, 2, 0)).reshape(block * chans, seqs)
    hbm = pl.BlockSpec(memory_space=pltpu.HBM)
    dma = pltpu.SemaphoreType.DMA
    return pl.pallas_call(
        kernel,
        out_shape=pltpu.VMEM((192, NJ, CZ), BF16),
        in_specs=[hbm] * 5,
        out_specs=pl.BlockSpec(memory_space=pltpu.VMEM),
        scratch_shapes=[
            pltpu.VMEM((3, 2, 4, 4, PART, LANES), BF16),
            pltpu.VMEM((4, 2, ROWS, LANES), BF16),
            pltpu.VMEM((ROWS, LANES), BF16),
            pltpu.VMEM((ROWS, LANES), BF16),
            pltpu.VMEM((ROWS, LANES), BF16),
            pltpu.VMEM((256, 256), jnp.int32),
            pltpu.VMEM((256, 256), jnp.int32),
            pltpu.VMEM((2, 256, LANES), F32),
            pltpu.VMEM((2, 256, LANES), F32),
            pltpu.VMEM((2, SPAN, LANES), F32),
            pltpu.VMEM((1024, CZ), BF16),
            pltpu.VMEM((1, CZ), F32),
            pltpu.VMEM((2, CZ, 512), BF16),
            pltpu.VMEM((256, 256), BF16),
            pltpu.VMEM((CHAN, SPAN, 256), BF16),
            pltpu.VMEM((2, 768, 256), BF16),
            pltpu.VMEM((2, 768, 2048), BF16),
            pltpu.VMEM((NJ, 128), F32),
            pltpu.VMEM((3, NJ // 2, 128), F32),
            pltpu.VMEM((SPAN * STRIDE, CZ), F32),
            dma((6,)),
            dma((4, 4)),
            dma((4, 2, 3)),
            dma((3,)),
            dma((3,)),
            dma((3, 3)),
            dma((3, 3)),
            dma((3, 2, 3)),
            dma((3, 2, 3)),
            dma((3,)),
            dma((3,)),
        ],
        compiler_params=pltpu.CompilerParams(
            collective_id=0, has_side_effects=True, vmem_limit_bytes=52 * 2**20
        ),
        cost_estimate=pl.CostEstimate(flops=7 * 10**9, bytes_accessed=5 * 10**6, transcendentals=0),
    )(a, b, coverage, matrix, offset.reshape(1, CZ))


def solution(mesh):
    in_specs = (P("seq", ("row", "col"), None), P("seq", ("col", "row"), None), P(), P(), P())
    out_specs = P("row", ("col", "seq"), None)
    return jax.shard_map(local, mesh=mesh, in_specs=in_specs, out_specs=out_specs, check_vma=False)
```

time: 282 us -> 43.4 us (0.15)
  matrix products: 76.1 us -> 0 us
  local copies, waits for them, and re-layouts: 68 us -> 1.41 us
  blocking collectives: 59.9 us -> 0 us
  waiting for transfers between devices: 52.4 us -> 0 us
  Pallas kernels: 0 us -> 41.9 us
  between operations: 13.5 us -> 0.01 us
  other arithmetic: 7.17 us -> 0 us
  loops' own time: 4.22 us -> 0 us
    dot_general x13 -> x0, matrix products: 76.1 us -> none  [the longest x6 41.5 us: pair_rows(): jnp.dot(product, final_linear_matrix, preferred_element_type=jnp.float32)]
    convert_element_type x6 -> x0, local copies, waits for them, and re-layouts: 63.6 us -> none  [pair_rows(): product.reshape(row_count * col_count, chan_count * chan_count)]
    all_gather x1 -> x0, blocking collectives: 59.9 us -> none  [local(): lax.all_gather(second_linear_features, 'row', axis=1, tiled=True)]
    pallas_call x0 -> x1, Pallas kernels: none -> 41.9 us  [local(): pl.pallas_call(kernel, out_shape=pltpu.VMEM((192, NJ, CZ), BF16), in_spec...]
    reduce_scatter x1 -> x0, waiting for transfers between devices: 29.7 us -> none  [local(): lax.psum_scatter(partial_sum, 'seq', scatter_dimension=1, tiled=True)]
    all_gather x1 -> x0, waiting for transfers between devices: 22.1 us -> none  [local(): lax.all_gather(first_linear_features, 'col', axis=1, tiled=True)]
    convert_element_type x2 -> x0, other arithmetic: 5.58 us -> none  [the longest x1 4.07 us: local(): ((summed + final_offset_vector) / jnp.maximum(counts, 1.0)[:, :, None]).a...]
    dynamic_slice x10 -> x0, local copies, waits for them, and re-layouts: 4.36 us -> none  [the longest x6 3.95 us: project_pairs(): lax.map(one_slab, jnp.arange(row_count // row_step, dtype=jnp.int32))]
  transfers between devices with their start and end apart: 2 -> 0, of which waited for: 2 -> 0; matrix products, arithmetic and copies ran while one was open for 1% -> 0% of each run, Pallas kernels for 0% -> 0%
where the time goes in v2:
time: 43.4 us; the launch traced here: 43.3 us
  Pallas kernels  41.9 us (97%)
  local copies, waits for them, and re-layouts  1.41 us (3%)
    pallas_call x1, Pallas kernels, local(): pl.pallas_call(kernel, out_shape=pltpu.VMEM((192, NJ, CZ), BF16), in_spec...  41.9 us
    unnamed x1, local copies, waits for them, and re-layouts  1.41 us

profile of v2, /device:TPU:1, one launch (start us, length us, event | category | flops | bytes accessed | tf_op | source)
XLA Modules:
  0.0 43.3 jit_solution(8549851395455346429)
XLA Ops:
  0.0 41.9 %shard_map.55 = bf16[192,48,128]{2,1,0:T(8,128)(2,1)S(1)} custom-call(bf16[384,128]{1,0:T(8,128)(2,1)} %bitcast.7, bf16[384,128]{1,0:T(8,128)(2,1)} %bitcast.8, s32[256,1536]{1,0:T(8,128)} %m_hbm.1, bf16[1024,128]{1,0:T(8,128)(2,1)} %w_hbm.1, f32[1,128]{1,0:T(1,128)} %bitcast.9), custom_call_target="tpu_custom_call" | custom-call | flops 7000000000 | bytes 5000000 | tf_op jit(solution)/shard_map/pallas_call | solution.py:324
  41.9 1.4 %copy.7 = bf16[192,48,128]{2,1,0:T(8,128)(2,1)} copy(bf16[192,48,128]{2,1,0:T(8,128)(2,1)S(1)} %shard_map.55) | data formatting | bytes 4718592

commit v3 on v2

--- a/solution.py
+++ b/solution.py
@@ -13,7 +13,6 @@
 BLK = 12
 ROWS = BLK * CHAN
 PART = 4 * CHAN
-HALF = PART // 2
 LANES = 128
 NJ = 48
 CZ = 128
@@ -136,9 +135,9 @@
             src_ref=src, dst_ref=dst, send_sem=send_sem, recv_sem=recv_sem, device_id=device, device_id_type=MESH
         )
 
-    def to_core(r):
-        piece = a_all.at[r, k]
-        return remote(piece, piece, csend.at[r], crecv.at[r], (1 - k, row, col))
+    def to_core(r, dy):
+        piece = a_all.at[r, k, dy]
+        return remote(piece, piece, csend.at[r, dy], crecv.at[r, dy], (1 - k, row, col))
 
     def to_z(r, g):
         return remote(
@@ -165,15 +164,17 @@
             arrived(a_all.at[r, k, 0, g], zrecv.at[r, g - 1])
         for dy in (3, 1, 2):
             to_y(r, 1, dy).start()
+        to_core(r, 0).start()
 
     def stage_b(r):
         for dy in (1, 2, 3):
             arrived(a_all.at[r, k, dy, pl.ds(0, 1)], yrecv.at[r, 0, dy - 1])
             arrived(a_all.at[r, k, dy, pl.ds(1, 3)], yrecv.at[r, 1, dy - 1])
-        to_core(r).start()
+            to_core(r, dy).start()
 
     def gathered(r):
-        arrived(a_all.at[r, 1 - k], crecv.at[r])
+        for dy in range(4):
+            arrived(a_all.at[r, 1 - k, dy], crecv.at[r, dy])
 
     origin_col = [(zl ^ g) * 4 + yy for yy in (y, ym, yp, (y + 2) % 4) for g in range(4)]
 
@@ -184,8 +185,6 @@
         for dy in (3, 1, 2):
             to_y(r, 0, dy).start()
     b_spread(None)
-    z_send(1)
-    z_send(2)
 
     loads[4].wait()
     loads[5].wait()
@@ -211,13 +210,14 @@
             recips[r, :, pl.ds(odd * SPAN, SPAN)] = recip_tmp[pl.ds(odd, NJ // 2, stride=2), :][:, 0:SPAN]
 
     stage_a(0)
-    stage_a(1)
-    stage_a(2)
+    z_send(1)
     for h in range(3):
         far[h].wait_recv()
         b_spread(h)
+    z_send(2)
+    stage_a(1)
     stage_b(0)
-    stage_b(1)
+    stage_a(2)
 
     def prepare_b():
         for xx in range(2):
@@ -286,7 +286,7 @@
                 i = c * 4 + n
                 o_ref[origin_col[c] * BLK + r * 4 + n] = staged[pl.ds(i * STRIDE, NJ), :].astype(BF16)
 
-    events = {(0, 10): lambda: stage_b(2)}
+    events = {(0, 12): lambda: stage_b(1), (1, 10): lambda: stage_b(2)}
     prepare_b()
     for r in range(3):
         gathered(r)
@@ -309,10 +309,11 @@
 
         to_z(r, 3).wait_send()
 
-        for rest in range(2):
-            for dy in (1, 2, 3):
+        for dy in (1, 2, 3):
+            for rest in range(2):
                 to_y(r, rest, dy).wait_send()
-        to_core(r).wait_send()
+        for dy in range(4):
+            to_core(r, dy).wait_send()
 
 
 def local(first, second, coverage, matrix, offset):
@@ -356,8 +357,8 @@
             dma((3, 3)),
             dma((3, 2, 3)),
             dma((3, 2, 3)),
-            dma((3,)),
-            dma((3,)),
+            dma((3, 4)),
+            dma((3, 4)),
         ],
         compiler_params=pltpu.CompilerParams(
             collective_id=0, has_side_effects=True, vmem_limit_bytes=52 * 2**20

time: 43.4 us -> 41.5 us (0.956)
  Pallas kernels: 41.9 us -> 39.9 us
    pallas_call x1, Pallas kernels: 41.9 us -> 39.9 us  [local(): pl.pallas_call(kernel, out_shape=pltpu.VMEM((192, NJ, CZ), BF16), in_spec...]
where the time goes in v3:
time: 41.5 us; the launch traced here: 41.3 us
  Pallas kernels  39.9 us (96%)
  local copies, waits for them, and re-layouts  1.41 us (3%)
    pallas_call x1, Pallas kernels, local(): pl.pallas_call(kernel, out_shape=pltpu.VMEM((192, NJ, CZ), BF16), in_spec...  39.9 us
    unnamed x1, local copies, waits for them, and re-layouts  1.41 us

profile of v3, /device:TPU:1, one launch (start us, length us, event | category | flops | bytes accessed | tf_op | source)
XLA Modules:
  0.0 41.3 jit_solution(14111660124929666300)
XLA Ops:
  0.0 39.9 %shard_map.55 = bf16[192,48,128]{2,1,0:T(8,128)(2,1)S(1)} custom-call(bf16[384,128]{1,0:T(8,128)(2,1)} %bitcast.7, bf16[384,128]{1,0:T(8,128)(2,1)} %bitcast.8, s32[256,1536]{1,0:T(8,128)} %m_hbm.1, bf16[1024,128]{1,0:T(8,128)(2,1)} %w_hbm.1, f32[1,128]{1,0:T(1,128)} %bitcast.9), custom_call_target="tpu_custom_call" | custom-call | flops 7000000000 | bytes 5000000 | tf_op jit(solution)/shard_map/pallas_call | solution.py:325
  39.9 1.4 %copy.7 = bf16[192,48,128]{2,1,0:T(8,128)(2,1)} copy(bf16[192,48,128]{2,1,0:T(8,128)(2,1)S(1)} %shard_map.55) | data formatting | bytes 4718592

commit v4 on v3

--- a/solution.py
+++ b/solution.py
@@ -162,7 +162,7 @@
     def stage_a(r):
         for g in (1, 2, 3):
             arrived(a_all.at[r, k, 0, g], zrecv.at[r, g - 1])
-        for dy in (3, 1, 2):
+        for dy in (1, 2, 3):
             to_y(r, 1, dy).start()
         to_core(r, 0).start()
 
@@ -182,7 +182,7 @@
     for c in far:
         c.start()
     for r in range(3):
-        for dy in (3, 1, 2):
+        for dy in (1, 2, 3):
             to_y(r, 0, dy).start()
     b_spread(None)
 
@@ -286,7 +286,7 @@
                 i = c * 4 + n
                 o_ref[origin_col[c] * BLK + r * 4 + n] = staged[pl.ds(i * STRIDE, NJ), :].astype(BF16)
 
-    events = {(0, 12): lambda: stage_b(1), (1, 10): lambda: stage_b(2)}
+    events = {(0, 8): lambda: stage_b(1), (1, 1): lambda: stage_b(2)}
     prepare_b()
     for r in range(3):
         gathered(r)

time: 41.5 us -> 41.2 us (level)
  no operation moved by 1% of the time
where the time goes in v4:
time: 41.2 us; the launch traced here: 40.9 us
  Pallas kernels  39.5 us (96%)
  local copies, waits for them, and re-layouts  1.41 us (3%)
    pallas_call x1, Pallas kernels, local(): pl.pallas_call(kernel, out_shape=pltpu.VMEM((192, NJ, CZ), BF16), in_spec...  39.5 us
    unnamed x1, local copies, waits for them, and re-layouts  1.41 us

profile of v4, /device:TPU:1, one launch (start us, length us, event | category | flops | bytes accessed | tf_op | source)
XLA Modules:
  0.0 40.9 jit_solution(11652344298809965042)
XLA Ops:
  0.0 39.5 %shard_map.55 = bf16[192,48,128]{2,1,0:T(8,128)(2,1)S(1)} custom-call(bf16[384,128]{1,0:T(8,128)(2,1)} %bitcast.7, bf16[384,128]{1,0:T(8,128)(2,1)} %bitcast.8, s32[256,1536]{1,0:T(8,128)} %m_hbm.1, bf16[1024,128]{1,0:T(8,128)(2,1)} %w_hbm.1, f32[1,128]{1,0:T(1,128)} %bitcast.9), custom_call_target="tpu_custom_call" | custom-call | flops 7000000000 | bytes 5000000 | tf_op jit(solution)/shard_map/pallas_call | solution.py:325
  39.5 1.4 %copy.7 = bf16[192,48,128]{2,1,0:T(8,128)(2,1)} copy(bf16[192,48,128]{2,1,0:T(8,128)(2,1)S(1)} %shard_map.55) | data formatting | bytes 4718592
